TPU v7x, 32 devices: a whole 2x2x4 slice. The times are simulated.
32 devices in a mesh: mod: 2 (over y), dp: 16 (over z, x, core).
Axes of the slice: x: 2, y: 2, z: 4, core: 2. Of those that a mesh axis runs over, the one named last changes fastest.
Arguments:
- patch_tokens: bfloat16 [2, 32, 256, 768], P('mod', 'dp'), may hold values from -6 to 6
- grid_coords: int32 [32, 2, 256], P('dp'), may hold values from 0 to 15, as said below
- has_radar: int32 [32], P('dp'), may hold values 0 or 1
- enc_gains: float32 [2, 2, 768], P('mod'), may hold values from 0.1 to 1.9
- enc_project: bfloat16 [2, 768, 2304], P('mod'), may hold values from -0.21875 to 0.21875
- enc_mixer: bfloat16 [2, 768, 768], P('mod'), may hold values from -0.625 to 0.625
- enc_expand: bfloat16 [2, 768, 3072], P('mod'), may hold values from -0.21875 to 0.21875
- enc_reduce: bfloat16 [2, 3072, 768], P('mod'), may hold values from -0.109375 to 0.109375
- cross_norms: float32 [2, 768], replicated, may hold values from 0.1 to 1.9
- cross_gain: float32 [768], replicated, may hold values from 0.1 to 1.9
- cross_query: bfloat16 [768, 768], P(None, 'mod'), may hold values from -0.21875 to 0.21875
- cross_keyval: bfloat16 [2, 768, 768], P(None, None, 'mod'), may hold values from -0.21875 to 0.21875
- cross_mixer: bfloat16 [768, 768], P('mod'), may hold values from -0.625 to 0.625
- cross_expand: bfloat16 [768, 3072], P(None, 'mod'), may hold values from -0.21875 to 0.21875
- cross_reduce: bfloat16 [3072, 768], P('mod'), may hold values from -0.109375 to 0.109375
- enc_cotangent: bfloat16 [2, 32, 256, 768], P('mod', 'dp'), may hold values from -8 to 8
- joined_cotangent: bfloat16 [32, 256, 768], P('dp'), may hold values from -8 to 8
Outputs:
- encoded: bfloat16 [2, 32, 256, 768], P('mod', 'dp')
- joined_tokens: bfloat16 [32, 256, 768], P('dp')
- contrast_loss: float32 [], replicated
- patch_grad: float32 [2, 32, 256, 768], P('mod', 'dp')
- enc_gains_grad: float32 [2, 2, 768], P('mod', None, 'dp')
- enc_project_grad: float32 [2, 768, 2304], P('mod', 'dp')
- enc_mixer_grad: float32 [2, 768, 768], P('mod', 'dp')
- enc_expand_grad: float32 [2, 768, 3072], P('mod', 'dp')
- enc_reduce_grad: float32 [2, 3072, 768], P('mod', None, 'dp')
- cross_norms_grad: float32 [2, 768], P('mod', 'dp')
- cross_gain_grad: float32 [768], P('dp')
- cross_query_grad: float32 [768, 768], P('dp', 'mod')
- cross_keyval_grad: float32 [2, 768, 768], P(None, 'dp', 'mod')
- cross_mixer_grad: float32 [768, 768], P('mod', 'dp')
- cross_expand_grad: float32 [768, 3072], P('dp', 'mod')
- cross_reduce_grad: float32 [3072, 768], P('mod', 'dp')
Inputs may be any that keep to these rules, and one draw needn't show every extreme that they name: For each image, grid_coords[i, 0, j] and grid_coords[i, 1, j] are the grid row and column of patch j; each of the 16 x 16 cells appears exactly once per image.
All inputs are finite; a program needn't handle non-finite values. No bound on the sum of `has_radar` on one device may be relied on, other than what follows from the above.
Results may differ from a plain program's by a relative error of at most 0.025.
Values may be sent and summed in bfloat16 or wider, within the bound.
A program may use at most 192 MiB of HBM per device.

v0:
```python
import jax
import jax.numpy as jnp
from jax import lax
from jax.sharding import PartitionSpec as P

HEADS = 12
HEAD_DIM = 64


logit_scale = 50.0


def swapped(array, axis, bit):
    return lax.ppermute(array, axis, [(i, i ^ 1 << bit) for i in range(lax.axis_size(axis))])


def norm_forward(values, gain):
    centre = values - jnp.mean(values, axis=-1, keepdims=True)
    inverse = lax.rsqrt(jnp.mean(centre * centre, axis=-1, keepdims=True) + 1e-06)
    unit_rows = centre * inverse
    return (unit_rows * gain, unit_rows, inverse)


def norm_backward(grad_out, unit_rows, inverse, gain):
    weighted = grad_out * gain
    grad_in = inverse * (
        weighted
        - jnp.mean(weighted, axis=-1, keepdims=True)
        - unit_rows * jnp.mean(weighted * unit_rows, axis=-1, keepdims=True)
    )
    return (grad_in, jnp.sum(grad_out * unit_rows, axis=(0, 1)))


def matmul(left_side, right_side):
    return jnp.einsum("npd,de->npe", left_side, right_side, preferred_element_type=jnp.float32)


def matmul_back(left_side, right_side):
    return jnp.einsum("npe,de->npd", left_side, right_side, preferred_element_type=jnp.float32)


def weight_grad(inputs, grad_rows):
    return jnp.einsum("npd,npe->de", inputs, grad_rows, preferred_element_type=jnp.float32)


def gelu_grad(pre_act, upstream):
    return jax.vjp(jax.nn.gelu, pre_act)[1](upstream)[0]


def slopes_for(first_head, head_total):
    return jnp.exp2(-8.0 * (first_head + jnp.arange(head_total) + 1).astype(jnp.float32) / HEADS)


def split_heads(values, head_count):
    return values.reshape(values.shape[0], values.shape[1], head_count, HEAD_DIM)


def to_front(arrays, positions):
    return tuple((jnp.moveaxis(member, where, 0) for member, where in zip(arrays, positions)))


def from_front(arrays, positions):
    return tuple((jnp.moveaxis(member, 0, where) for member, where in zip(arrays, positions)))


def attend_forward(query_rows, key_rows, value_rows, bias):
    head_count = bias.shape[1]
    scores = (
        jnp.einsum(
            "nqhd,nkhd->nhqk",
            split_heads(query_rows, head_count),
            split_heads(key_rows, head_count),
            preferred_element_type=jnp.float32,
        )
        * HEAD_DIM ** (-0.5)
        + bias
    )
    highest = jnp.max(scores, axis=-1, keepdims=True)
    shifted = jnp.exp(scores - highest)
    denominator = jnp.sum(shifted, axis=-1, keepdims=True)
    probabilities = (shifted / denominator).astype(jnp.bfloat16)
    mixed_heads = jnp.einsum(
        "nhqk,nkhd->nqhd",
        probabilities,
        split_heads(value_rows, head_count),
        preferred_element_type=jnp.float32,
    )
    log_total = (highest + jnp.log(denominator))[..., 0]
    return (mixed_heads.reshape(query_rows.shape).astype(jnp.bfloat16), log_total)


def attend_backward(query_rows, key_rows, value_rows, bias, log_total, grad_mixed):
    head_count = bias.shape[1]
    query_heads = split_heads(query_rows, head_count)
    key_heads = split_heads(key_rows, head_count)
    value_heads = split_heads(value_rows, head_count)
    grad_heads = split_heads(grad_mixed, head_count)
    scale_factor = HEAD_DIM ** (-0.5)
    scores = (
        jnp.einsum("nqhd,nkhd->nhqk", query_heads, key_heads, preferred_element_type=jnp.float32)
        * scale_factor
        + bias
    )
    probabilities = jnp.exp(scores - log_total[..., None])
    grad_probs = jnp.einsum(
        "nqhd,nkhd->nhqk", grad_heads, value_heads, preferred_element_type=jnp.float32
    )
    grad_values = jnp.einsum(
        "nhqk,nqhd->nkhd",
        probabilities.astype(jnp.bfloat16),
        grad_heads,
        preferred_element_type=jnp.float32,
    )
    inner_sum = jnp.sum(grad_probs * probabilities, axis=-1, keepdims=True)
    grad_scores = (probabilities * (grad_probs - inner_sum)).astype(jnp.bfloat16)
    grad_queries = (
        jnp.einsum("nhqk,nkhd->nqhd", grad_scores, key_heads, preferred_element_type=jnp.float32)
        * scale_factor
    )
    grad_keys = (
        jnp.einsum("nhqk,nqhd->nkhd", grad_scores, query_heads, preferred_element_type=jnp.float32)
        * scale_factor
    )
    row_shape = query_rows.shape
    return (
        grad_queries.reshape(row_shape),
        grad_keys.reshape(row_shape),
        grad_values.reshape(row_shape),
    )


def contrast(pooled, present):
    unit_rows = pooled * lax.rsqrt(jnp.mean(pooled * pooled, axis=-1, keepdims=True) + 1e-06)
    logits = jnp.dot(unit_rows[0], unit_rows[1].T, precision=lax.Precision.HIGHEST) * (
        logit_scale / pooled.shape[2]
    )
    absent = 10000.0 * (1.0 - present)
    row_total = jax.nn.logsumexp(logits - absent[None, :], axis=1)
    column_total = jax.nn.logsumexp(logits - absent[:, None], axis=0)
    return jnp.sum(present * (row_total + column_total - 2.0 * jnp.diagonal(logits))) / (
        2.0 * pooled.shape[1]
    )


def shards(
    patch_tokens,
    grid_coords,
    has_radar,
    enc_gains,
    enc_project,
    enc_mixer,
    enc_expand,
    enc_reduce,
    cross_norms,
    cross_gain,
    cross_query,
    cross_keyval,
    cross_mixer,
    cross_expand,
    cross_reduce,
    enc_cotangent,
    joined_cotangent,
):
    item_count = patch_tokens.shape[1]
    patches = patch_tokens.shape[2]
    model_width = patch_tokens.shape[3]
    half_index = lax.axis_index("mod")
    is_radar = half_index == 1
    grid_rows = grid_coords[:, 0, :].astype(jnp.float32)
    grid_columns = grid_coords[:, 1, :].astype(jnp.float32)
    across = grid_rows[:, :, None] - grid_rows[:, None, :]
    upward = grid_columns[:, :, None] - grid_columns[:, None, :]
    distance = jnp.sqrt(across * across + upward * upward)
    full_bias = -slopes_for(0, HEADS)[None, :, None, None] * distance[:, None]
    local_heads = cross_query.shape[1] // HEAD_DIM
    cross_bias = (
        -slopes_for(half_index * local_heads, local_heads)[None, :, None, None] * distance[:, None]
    )
    tokens = patch_tokens[0].astype(jnp.float32)
    gain_pair = enc_gains[0]
    normed, unit_one, inverse_one = norm_forward(tokens, gain_pair[0])
    normed = normed.astype(jnp.bfloat16)
    project = matmul(normed, enc_project[0]).astype(jnp.bfloat16)
    query_rows = project[..., :model_width]
    key_rows = project[..., model_width : 2 * model_width]
    value_rows = project[..., 2 * model_width :]
    mixed_heads, log_total = attend_forward(query_rows, key_rows, value_rows, full_bias)
    residual = tokens + matmul(mixed_heads, enc_mixer[0])
    normed_two, unit_two, inverse_two = norm_forward(residual, gain_pair[1])
    normed_two = normed_two.astype(jnp.bfloat16)
    expanded = matmul(normed_two, enc_expand[0])
    hidden = jax.nn.gelu(expanded).astype(jnp.bfloat16)
    encoded = (residual + matmul(hidden, enc_reduce[0])).astype(jnp.bfloat16)
    partner = swapped(encoded, "mod", 0)
    radar_tokens = jnp.where(is_radar, encoded, partner).astype(jnp.float32)
    optical = jnp.where(is_radar, partner, encoded).astype(jnp.float32)
    query_in, unit_query, inverse_query = norm_forward(radar_tokens, cross_norms[1])
    keyval_in, unit_keyval, inverse_keyval = norm_forward(optical, cross_norms[0])
    query_in = query_in.astype(jnp.bfloat16)
    keyval_in = keyval_in.astype(jnp.bfloat16)
    cross_queries = matmul(query_in, cross_query).astype(jnp.bfloat16)
    cross_keys = matmul(keyval_in, cross_keyval[0]).astype(jnp.bfloat16)
    cross_values = matmul(keyval_in, cross_keyval[1]).astype(jnp.bfloat16)
    cross_mixed, cross_total = attend_forward(cross_queries, cross_keys, cross_values, cross_bias)
    attention = lax.psum(matmul(cross_mixed, cross_mixer).astype(jnp.bfloat16), "mod").astype(
        jnp.float32
    )
    cross_resid = radar_tokens + attention
    cross_normed, unit_cross, inverse_cross = norm_forward(cross_resid, cross_gain)
    cross_normed = cross_normed.astype(jnp.bfloat16)
    cross_expanded = matmul(cross_normed, cross_expand)
    cross_hidden = jax.nn.gelu(cross_expanded).astype(jnp.bfloat16)
    branch = lax.psum(matmul(cross_hidden, cross_reduce).astype(jnp.bfloat16), "mod").astype(
        jnp.float32
    )
    present = has_radar.astype(jnp.float32)[:, None, None]
    joined_tokens = (present * (cross_resid + branch)).astype(jnp.bfloat16)
    pooled_own = jnp.mean(encoded.astype(jnp.float32), axis=1)
    whole_pool, whole_present = (
        lax.all_gather(pooled_own, ("mod", "dp"), axis=0, tiled=True),
        lax.all_gather(has_radar, ("mod", "dp"), axis=0, tiled=True),
    )
    total_items = whole_pool.shape[0] // 2
    pooled_all = whole_pool.reshape(2, total_items, model_width)
    present_all = whole_present[:total_items].astype(jnp.float32)
    loss_value, pullback = jax.vjp(lambda pooled: contrast(pooled, present_all), pooled_all)
    pool_grad = pullback(jnp.ones_like(loss_value))[0]
    own_pool_grad = lax.dynamic_slice(
        pool_grad, (half_index, lax.axis_index("dp") * item_count, 0), (1, item_count, model_width)
    )[0]
    grad_joined = present * joined_cotangent.astype(jnp.float32)
    grad_branch = grad_joined.astype(jnp.bfloat16)
    creduce_grad = weight_grad(cross_hidden, grad_branch)
    grad_chidden = matmul_back(grad_branch, cross_reduce)
    grad_cexpanded = gelu_grad(cross_expanded, grad_chidden).astype(jnp.bfloat16)
    cexpand_grad = weight_grad(cross_normed, grad_cexpanded)
    grad_cnormed = lax.psum(
        matmul_back(grad_cexpanded, cross_expand).astype(jnp.bfloat16), "mod"
    ).astype(jnp.float32)
    grad_cresid, gain_grad = norm_backward(grad_cnormed, unit_cross, inverse_cross, cross_gain)
    grad_cresid = grad_joined + grad_cresid
    grad_attention = grad_cresid.astype(jnp.bfloat16)
    cmixer_grad = weight_grad(cross_mixed, grad_attention)
    grad_cmixed = matmul_back(grad_attention, cross_mixer).astype(jnp.bfloat16)
    grad_cq, grad_ck, grad_cv = attend_backward(
        cross_queries, cross_keys, cross_values, cross_bias, cross_total, grad_cmixed
    )
    grad_cq = grad_cq.astype(jnp.bfloat16)
    grad_ck = grad_ck.astype(jnp.bfloat16)
    grad_cv = grad_cv.astype(jnp.bfloat16)
    query_grad = weight_grad(query_in, grad_cq)
    keyval_grad = jnp.stack([weight_grad(keyval_in, grad_ck), weight_grad(keyval_in, grad_cv)])
    grad_query_in = matmul_back(grad_cq, cross_query)
    grad_keyval_in = matmul_back(grad_ck, cross_keyval[0]) + matmul_back(grad_cv, cross_keyval[1])
    outgoing = jnp.where(is_radar, grad_keyval_in, grad_query_in)
    incoming = swapped(outgoing.astype(jnp.bfloat16), "mod", 0).astype(outgoing.dtype)
    own_norm_in = jnp.where(is_radar, grad_query_in, grad_keyval_in) + incoming
    own_unit = jnp.where(is_radar, unit_query, unit_keyval)
    own_inverse = jnp.where(is_radar, inverse_query, inverse_keyval)
    own_gain = jnp.where(is_radar, cross_norms[1], cross_norms[0])
    grad_own_norm, norms_grad = norm_backward(own_norm_in, own_unit, own_inverse, own_gain)
    norms_grad = norms_grad[None]
    cross_set = (
        norms_grad,
        gain_grad,
        query_grad,
        keyval_grad,
        cmixer_grad,
        cexpand_grad,
        creduce_grad,
    )
    cross_dims = (1, 0, 0, 1, 1, 0, 1)
    grad_out = (
        enc_cotangent[0].astype(jnp.float32)
        + own_pool_grad[:, None, :] / patches
        + grad_own_norm
        + jnp.where(is_radar, grad_cresid, 0.0)
    )
    grad_narrow = grad_out.astype(jnp.bfloat16)
    reduce_grad = weight_grad(hidden, grad_narrow)[None]
    grad_hidden = matmul_back(grad_narrow, enc_reduce[0])
    grad_expanded = gelu_grad(expanded, grad_hidden).astype(jnp.bfloat16)
    expand_grad = weight_grad(normed_two, grad_expanded)[None]
    grad_normed_two = matmul_back(grad_expanded, enc_expand[0])
    grad_resid, gain_two = norm_backward(grad_normed_two, unit_two, inverse_two, gain_pair[1])
    grad_resid = grad_out + grad_resid
    grad_mixer_out = grad_resid.astype(jnp.bfloat16)
    mixer_grad = weight_grad(mixed_heads, grad_mixer_out)[None]
    grad_mixed = matmul_back(grad_mixer_out, enc_mixer[0]).astype(jnp.bfloat16)
    grad_queries, grad_keys, grad_values = attend_backward(
        query_rows, key_rows, value_rows, full_bias, log_total, grad_mixed
    )
    grad_project = jnp.concatenate([grad_queries, grad_keys, grad_values], axis=-1).astype(
        jnp.bfloat16
    )
    project_grad = weight_grad(normed, grad_project)[None]
    grad_normed = matmul_back(grad_project, enc_project[0])
    grad_tokens, gain_one = norm_backward(grad_normed, unit_one, inverse_one, gain_pair[0])
    patch_grad = (grad_resid + grad_tokens)[None]
    gains_grad = jnp.stack([gain_one, gain_two])[None]
    encoder_set = (gains_grad, project_grad, mixer_grad, expand_grad, reduce_grad)
    encoder_dims = (2, 1, 1, 1, 2)
    every_dims = encoder_dims + cross_dims
    every_front = to_front(encoder_set + cross_set, every_dims)
    every_summed = (
        lax.psum_scatter(every_front[0], "dp", scatter_dimension=0, tiled=True),
        lax.psum_scatter(every_front[1], "dp", scatter_dimension=0, tiled=True),
        lax.psum_scatter(every_front[2], "dp", scatter_dimension=0, tiled=True),
        lax.psum_scatter(every_front[3], "dp", scatter_dimension=0, tiled=True),
        lax.psum_scatter(every_front[4], "dp", scatter_dimension=0, tiled=True),
        lax.psum_scatter(every_front[5], "dp", scatter_dimension=0, tiled=True),
        lax.psum_scatter(every_front[6], "dp", scatter_dimension=0, tiled=True),
        lax.psum_scatter(every_front[7], "dp", scatter_dimension=0, tiled=True),
        lax.psum_scatter(every_front[8], "dp", scatter_dimension=0, tiled=True),
        lax.psum_scatter(every_front[9], "dp", scatter_dimension=0, tiled=True),
        lax.psum_scatter(every_front[10], "dp", scatter_dimension=0, tiled=True),
        lax.psum_scatter(every_front[11], "dp", scatter_dimension=0, tiled=True),
    )
    (
        gains_sum,
        project_sum,
        mixer_sum,
        expand_sum,
        reduce_sum,
        norms_sum,
        gain_sum,
        query_sum,
        keyval_sum,
        cmixer_sum,
        cexpand_sum,
        creduce_sum,
    ) = from_front(every_summed, every_dims)
    return (
        encoded[None],
        joined_tokens,
        loss_value,
        patch_grad,
        gains_sum,
        project_sum,
        mixer_sum,
        expand_sum,
        reduce_sum,
        norms_sum,
        gain_sum,
        query_sum,
        keyval_sum,
        cmixer_sum,
        cexpand_sum,
        creduce_sum,
    )


def solution(mesh):
    placed = (
        P("mod", "dp", None, None),
        P("dp", None, None),
        P("dp"),
        P("mod", None, None),
        P("mod", None, None),
        P("mod", None, None),
        P("mod", None, None),
        P("mod", None, None),
        P(),
        P(),
        P(None, "mod"),
        P(None, None, "mod"),
        P("mod", None),
        P(None, "mod"),
        P("mod", None),
        P("mod", "dp", None, None),
        P("dp", None, None),
    )
    return jax.shard_map(
        shards,
        mesh=mesh,
        in_specs=placed,
        out_specs=(
            P("mod", "dp", None, None),
            P("dp", None, None),
            P(),
            P("mod", "dp", None, None),
            P("mod", None, "dp"),
            P("mod", "dp", None),
            P("mod", "dp", None),
            P("mod", "dp", None),
            P("mod", None, "dp"),
            P("mod", "dp"),
            P("dp"),
            P("dp", "mod"),
            P(None, "dp", "mod"),
            P("mod", "dp"),
            P("dp", "mod"),
            P("mod", "dp"),
        ),
        check_vma=False,
    )
```

profile of v0, /device:TPU:0, one launch (start us, length us, event | category | flops | bytes accessed | tf_op | source)
XLA Modules:
  0.0 1247.3 jit_solution(14902688606084755972)
XLA Ops:
  34.4 5.2 add_convert_fusion
  44.3 50.8 %all-reduce.2 = s32[64]{0:T(128)S(1)} all-reduce(s32[64]{0:T(128)} %dynamic-update-slice), channel_id=1, replica_groups=mesh['mod'=2,'dp'=16] {'mod','dp'}, use_global_device_ids=true, to_apply=%add.2 | all-reduce | flops 64 | bytes 512
  120.2 42.9 %all-gather = f32[32,2,768]{2,1,0:T(2,128)} all-gather(f32[1,2,768]{2,1,0:T(2,128)S(1)} %multiply_bitcast_fusion), channel_id=1, replica_groups=mesh['mod'=2,'dp'=16] {'mod','dp'}, dimensions={0}, use_global_device_ids=true | all-gather | bytes 202752 | tf_op jit(solution)/shard_map/all_gather | solution.py:220
  193.4 5.0 scatter_fusion
  199.1 33.0 %all-reduce.14.cloned.1.call-done = (bf16[2,256,768]{2,1,0:T(8,128)(2,1)}, bf16[2,256,768]{2,1,0:T(8,128)(2,1)}) async-done(((bf16[2,256,768]{2,1,0:T(8,128)(2,1)}, bf16[2,256,768]{2,1,0:T(8,128)(2,1)}), (bf16[2,256,768]{2,1,0:T(8,128)(2,1)}, bf16[2,256,768]{2,1,0:T(8,128)(2,1)})) %all-reduce.14.cloned.1.call-update) | async-done | bytes 1572880 | tf_op jit(solution)/shard_map/psum | solution.py:213
  232.2 4.4 fusion.76
  252.6 18.1 %collective-permute-done.1 = bf16[2,256,768]{2,1,0:T(8,128)(2,1)S(1)} collective-permute-done((bf16[2,256,768]{2,1,0:T(8,128)(2,1)S(1)}, bf16[2,256,768]{2,1,0:T(8,128)(2,1)S(1)}, u32[]{:S(2)}, u32[]{:S(2)}) %collective-permute-start.1) | collective-permute-done | bytes 786464 | tf_op jit(solution)/shard_map/ppermute | solution.py:14
  275.0 6.4 fusion.6
  281.5 3.5 multiply_reduce_fusion.3
  290.8 5.1 fusion.96
  295.8 6.9 multiply_reduce_fusion
  302.8 4.5 multiply_convert_fusion
  320.4 5.8 fusion.68
  328.5 10.1 convolution_bitcast_fusion.1
  338.7 20.7 %copy.144 = f32[768,1,3072]{2,1,0:T(1,128)} copy(f32[768,1,3072]{0,2,1:T(8,128)} %convolution_bitcast_fusion.1) | data formatting | bytes 18874368 | tf_op jit(solution)/shard_map/transpose | solution.py:59
  359.5 4.2 convolution_bitcast_fusion.6
  371.6 3.9 convolution_bitcast_fusion.5
  376.2 5.9 convolution_bitcast_fusion.3
  382.7 5.6 convolution_bitcast_fusion.4
  389.0 6.9 convolution_bitcast_fusion
  396.0 8.9 convolution_bitcast_fusion.2
  407.4 33.0 %all-reduce.4 = f32[768]{0:T(1024)} all-reduce(f32[768]{0:T(1024)S(1)} %copy-done.93), channel_id=8, replica_groups=mesh['mod'=2,'dp'=16] {'dp'}, use_global_device_ids=true, to_apply=%region_46.47.clone | all-reduce | flops 768 | bytes 6144
  443.0 3.8 fusion.67
  449.6 164.3 %all-reduce.12.cloned.1.call-done = f32[768,1,3072]{2,1,0:T(1,128)} async-done(((f32[768,1,3072]{2,1,0:T(1,128)}), f32[768,1,3072]{2,1,0:T(1,128)}) %all-reduce.12.cloned.1.call-update) | async-done | bytes 9437200
  615.9 60.5 %reduce-scatter.25.cloned.1.call-done = f32[48,384]{1,0:T(8,128)} async-done(((f32[768,384]{1,0:T(8,128)}), f32[48,384]{1,0:T(8,128)}) %reduce-scatter.25.cloned.1.call-update) | async-done | bytes 73744 | tf_op jit(solution)/shard_map/reduce_scatter | solution.py:315
  676.4 61.8 %reduce-scatter.21.cloned.1.call-done = f32[48,384]{1,0:T(8,128)} async-done(((f32[768,384]{1,0:T(8,128)}), f32[48,384]{1,0:T(8,128)}) %reduce-scatter.21.cloned.1.call-update) | async-done | bytes 73744 | tf_op jit(solution)/shard_map/reduce_scatter | solution.py:313
  738.2 66.8 %reduce-scatter.23.cloned.1.call-done = f32[48,2,384]{2,0,1:T(8,128)} async-done(((f32[768,2,384]{2,0,1:T(8,128)}), f32[48,2,384]{2,0,1:T(8,128)}) %reduce-scatter.23.cloned.1.call-update) | async-done | bytes 147472 | tf_op jit(solution)/shard_map/reduce_scatter | solution.py:314
  805.0 66.4 %reduce-scatter.17.cloned.1.call-done = f32[48,1,768]{2,0,1:T(8,128)} async-done(((f32[768,1,768]{2,0,1:T(8,128)}), f32[48,1,768]{2,0,1:T(8,128)}) %reduce-scatter.17.cloned.1.call-update) | async-done | bytes 147472 | tf_op jit(solution)/shard_map/reduce_scatter | solution.py:308
  871.4 79.4 %reduce-scatter.29.cloned.1.call-done = f32[48,1536]{1,0:T(8,128)} async-done(((f32[768,1536]{1,0:T(8,128)}), f32[48,1536]{1,0:T(8,128)}) %reduce-scatter.29.cloned.1.call-update) | async-done | bytes 294928 | tf_op jit(solution)/shard_map/reduce_scatter | solution.py:317
  950.8 79.1 %reduce-scatter.27.cloned.1.call-done = f32[48,1536]{1,0:T(8,128)} async-done(((f32[768,1536]{1,0:T(8,128)}), f32[48,1536]{1,0:T(8,128)}) %reduce-scatter.27.cloned.1.call-update) | async-done | bytes 294928 | tf_op jit(solution)/shard_map/reduce_scatter | solution.py:316
  1029.9 94.1 %reduce-scatter.15.cloned.1.call-done = f32[48,1,2304]{2,0,1:T(8,128)} async-done(((f32[768,1,2304]{2,0,1:T(8,128)}), f32[48,1,2304]{2,0,1:T(8,128)}) %reduce-scatter.15.cloned.1.call-update) | async-done | bytes 442384 | tf_op jit(solution)/shard_map/reduce_scatter | solution.py:307
  1124.0 115.5 %reduce-scatter.19.cloned.1.call-done = f32[48,1,3072]{2,0,1:T(8,128)} async-done(((f32[768,1,3072]{2,0,1:T(8,128)}), f32[48,1,3072]{2,0,1:T(8,128)}) %reduce-scatter.19.cloned.1.call-update) | async-done | bytes 589840 | tf_op jit(solution)/shard_map/reduce_scatter | solution.py:309
  (425 shorter events, 146.7 us)
Async XLA Ops:
  7.2 160.1 %all-reduce.10.cloned.1.call-start = ((), (), s32[]{:S(2)}) async-start(), calls=%async_computation.10 | async-start | bytes 1572864 | tf_op jit(solution)/shard_map/psum | solution.py:205
  10.4 20.6 %copy-start.56 = (f32[768]{0:T(1024)}, f32[768]{0:T(1024)S(1)}, u32[]{:S(2)}) copy-start(f32[768]{0:T(1024)S(1)} %get-tuple-element.88) | copy-start | bytes 9220
  34.4 8.7 copy-start.116
  34.4 60.7 %copy-start.104 = (f32[2,768]{1,0:T(2,128)S(1)}, f32[2,768]{1,0:T(2,128)}, u32[]{:S(2)}) copy-start(f32[2,768]{1,0:T(2,128)} %param.25) | copy-start | bytes 18436
  39.5 58.1 %collective-permute-start = (bf16[2,256,768]{2,1,0:T(8,128)(2,1)}, bf16[2,256,768]{2,1,0:T(8,128)(2,1)}, u32[]{:S(2)}, u32[]{:S(2)}) collective-permute-start(bf16[2,256,768]{2,1,0:T(8,128)(2,1)} %add_convert_fusion), channel_id=1, source_target_pairs={{0,16},{16,0},{1,17},{17,1},{2,18},{18,2},{3,19},{19,3},{4,20},{20... | collective-permute-start | bytes 2359304 | tf_op jit(solution)/shard_map/ppermute | solution.py:14
  95.1 9.6 copy-start.89
  118.5 113.6 %all-reduce.14.cloned.1.call-start = ((), (), s32[]{:S(2)}) async-start(), calls=%async_computation.22 | async-start | bytes 3145728 | tf_op jit(solution)/shard_map/psum | solution.py:213
  183.0 263.8 %reduce-scatter.33.cloned.1.call-start = ((), (), s32[]{:S(2)}) async-start(), calls=%async_computation.20 | async-start | bytes 417792
  244.7 30.2 %slice-start.10 = ((s8[6291456]{0:T(1024)(128)(4,1)}), s8[4194304]{0:T(1024)(128)(4,1)S(1)}, s32[]{:S(2)}) async-start(s8[6291456]{0:T(1024)(128)(4,1)} %bitcast.308), calls=%async_computation.33 | async-start | bytes 8388608
  249.9 25.0 %slice-start.11 = ((s8[6291456]{0:T(1024)(128)(4,1)}), s8[2097152]{0:T(1024)(128)(4,1)S(1)}, s32[]{:S(2)}) async-start(s8[6291456]{0:T(1024)(128)(4,1)} %bitcast.308), calls=%async_computation.34 | async-start | bytes 4194304
  250.6 20.1 %copy-start.16 = (bf16[2,256,768]{2,1,0:T(8,128)(2,1)S(1)}, bf16[2,256,768]{2,1,0:T(8,128)(2,1)}, u32[]{:S(2)}) copy-start(bf16[2,256,768]{2,1,0:T(8,128)(2,1)} %copy-done.15) | copy-start | bytes 2359300
  250.6 20.1 %copy-start.65 = (f32[768]{0:T(1024)S(1)}, f32[768]{0:T(1024)}, u32[]{:S(2)}) copy-start(f32[768]{0:T(1024)} %broadcast_select_fusion.2) | copy-start | bytes 9220
  250.6 20.1 %copy-start.67 = (f32[2,256]{1,0:T(2,128)S(1)}, f32[2,256]{1,0:T(2,128)}, u32[]{:S(2)}) copy-start(f32[2,256]{1,0:T(2,128)} %copy-done.66) | copy-start | bytes 6148
  250.6 20.1 %copy-start.69 = (f32[2,256]{1,0:T(2,128)S(1)}, f32[2,256]{1,0:T(2,128)}, u32[]{:S(2)}) copy-start(f32[2,256]{1,0:T(2,128)} %copy-done.68) | copy-start | bytes 6148
  250.6 20.1 %copy-start.80 = (f32[2,256]{1,0:T(2,128)S(1)}, f32[2,256]{1,0:T(2,128)}, u32[]{:S(2)}) copy-start(f32[2,256]{1,0:T(2,128)} %copy-done.79) | copy-start | bytes 6148
  250.7 20.1 %copy-start.83 = (f32[2,256]{1,0:T(2,128)S(1)}, f32[2,256]{1,0:T(2,128)}, u32[]{:S(2)}) copy-start(f32[2,256]{1,0:T(2,128)} %copy-done.82) | copy-start | bytes 6148
  251.4 19.4 %copy-start.7 = (bf16[2,256,768]{2,1,0:T(8,128)(2,1)S(1)}, bf16[2,256,768]{2,1,0:T(8,128)(2,1)}, u32[]{:S(2)}) copy-start(bf16[2,256,768]{2,1,0:T(8,128)(2,1)} %copy-done.4) | copy-start | bytes 2359300
  251.4 19.3 %collective-permute-start.1 = (bf16[2,256,768]{2,1,0:T(8,128)(2,1)S(1)}, bf16[2,256,768]{2,1,0:T(8,128)(2,1)S(1)}, u32[]{:S(2)}, u32[]{:S(2)}) collective-permute-start(bf16[2,256,768]{2,1,0:T(8,128)(2,1)S(1)} %get-tuple-element.122), channel_id=1, source_target_pairs={{0,16},{16,0},{1,17},{17,1},{2,18},{18,2},{3,19},{19,3},{4,20},{20... | collective-permute-start | bytes 2359304 | tf_op jit(solution)/shard_map/ppermute | solution.py:14
  275.0 10.0 copy-start.23
  290.7 12.0 slice-start
  311.8 136.4 %reduce-scatter.31.cloned.1.call-start = ((), (), s32[]{:S(2)}) async-start(), calls=%async_computation.19 | async-start | bytes 417792
  328.5 285.4 %all-reduce.12.cloned.1.call-start = ((), (), s32[]{:S(2)}) async-start(), calls=%async_computation.21 | async-start | bytes 18874368
  359.4 317.0 %reduce-scatter.25.cloned.1.call-start = ((), (), s32[]{:S(2)}) async-start(), calls=%async_computation.16 | async-start | bytes 1253376 | tf_op jit(solution)/shard_map/reduce_scatter | solution.py:315
  363.7 374.5 %reduce-scatter.21.cloned.1.call-start = ((), (), s32[]{:S(2)}) async-start(), calls=%async_computation.14 | async-start | bytes 1253376 | tf_op jit(solution)/shard_map/reduce_scatter | solution.py:313
  366.9 438.2 %reduce-scatter.23.cloned.1.call-start = ((), (), s32[]{:S(2)}) async-start(), calls=%async_computation.15 | async-start | bytes 2506752 | tf_op jit(solution)/shard_map/reduce_scatter | solution.py:314
  371.6 499.8 %reduce-scatter.17.cloned.1.call-start = ((), (), s32[]{:S(2)}) async-start(), calls=%async_computation.12 | async-start | bytes 2506752 | tf_op jit(solution)/shard_map/reduce_scatter | solution.py:308
  375.5 575.3 %reduce-scatter.29.cloned.1.call-start = ((), (), s32[]{:S(2)}) async-start(), calls=%async_computation.18 | async-start | bytes 5013504 | tf_op jit(solution)/shard_map/reduce_scatter | solution.py:317
  382.1 647.8 %reduce-scatter.27.cloned.1.call-start = ((), (), s32[]{:S(2)}) async-start(), calls=%async_computation.17 | async-start | bytes 5013504 | tf_op jit(solution)/shard_map/reduce_scatter | solution.py:316
  388.4 735.6 %reduce-scatter.15.cloned.1.call-start = ((), (), s32[]{:S(2)}) async-start(), calls=%async_computation.11 | async-start | bytes 7520256 | tf_op jit(solution)/shard_map/reduce_scatter | solution.py:307
  396.0 843.5 %reduce-scatter.19.cloned.1.call-start = ((), (), s32[]{:S(2)}) async-start(), calls=%async_computation.13 | async-start | bytes 10027008 | tf_op jit(solution)/shard_map/reduce_scatter | solution.py:309
  404.9 38.1 %copy-start.86 = (f32[768]{0:T(1024)S(1)}, f32[768]{0:T(1024)}, u32[]{:S(2)}) copy-start(f32[768]{0:T(1024)} %copy-done.85) | copy-start | bytes 9220
  404.9 38.1 %copy-start.97 = (f32[2,256]{1,0:T(2,128)S(1)}, f32[2,256]{1,0:T(2,128)}, u32[]{:S(2)}) copy-start(f32[2,256]{1,0:T(2,128)} %copy-done.96) | copy-start | bytes 6148
  (116 other events, 355.0 us)
Sparse Core Ops, SparseCore 0:
  118.7 33.7 all-reduce.9
  183.1 48.9 all-reduce.13
  311.9 55.5 reduce-scatter.32
  371.8 54.5 reduce-scatter.30
  430.0 183.7 all-reduce.11
  618.3 58.0 reduce-scatter.24
  681.0 57.1 reduce-scatter.20
  743.0 61.9 reduce-scatter.22
  809.4 61.9 reduce-scatter.16
  876.2 74.5 reduce-scatter.28
  955.2 74.5 reduce-scatter.26
  1034.8 89.0 reduce-scatter.14
  1128.6 110.8 reduce-scatter.18
where the time goes:
time: 1260 us; the launch traced here: 1250 us
  waiting for transfers between devices  839 us (67%)
  matrix products  130 us (10%)
  blocking collectives  127 us (10%)
  local copies, waits for them, and re-layouts  78.6 us (6%)
  other arithmetic  50 us (4%)
  between operations  18.1 us (1%)
    unnamed x16, waiting for transfers between devices  164 us
    reduce_scatter x1, waiting for transfers between devices, shards(): lax.psum_scatter(every_front[3], 'dp', scatter_dimension=0, tiled=True)  116 us
    reduce_scatter x1, waiting for transfers between devices, shards(): lax.psum_scatter(every_front[1], 'dp', scatter_dimension=0, tiled=True)  94.1 us
    unnamed x2, blocking collectives  83.8 us
    reduce_scatter x1, waiting for transfers between devices, shards(): lax.psum_scatter(every_front[11], 'dp', scatter_dimension=0, tiled=True)  79.4 us
    reduce_scatter x1, waiting for transfers between devices, shards(): lax.psum_scatter(every_front[10], 'dp', scatter_dimension=0, tiled=True)  79.1 us
    reduce_scatter x1, waiting for transfers between devices, shards(): lax.psum_scatter(every_front[8], 'dp', scatter_dimension=0, tiled=True)  66.8 us
    reduce_scatter x1, waiting for transfers between devices, shards(): lax.psum_scatter(every_front[2], 'dp', scatter_dimension=0, tiled=True)  66.4 us
  transfers between devices with their start and end apart: 15, of which 11 were waited for; matrix products, arithmetic and copies ran while one was open for 10% of the time, Pallas kernels for 0%

commit v1 on v0

v1 whole, which is shorter than its diff:
```python
import jax
import jax.numpy as jnp
from jax import lax
from jax.sharding import PartitionSpec as P

HEADS = 12
HEAD_DIM = 64
LOGIT_SCALE = 50.0
F32 = jnp.float32
BF16 = jnp.bfloat16


def norm_forward(values, gain):
    centre = values - jnp.mean(values, axis=-1, keepdims=True)
    inverse = lax.rsqrt(jnp.mean(centre * centre, axis=-1, keepdims=True) + 1e-06)
    unit_rows = centre * inverse
    return (unit_rows * gain, unit_rows, inverse)


def norm_backward(grad_out, unit_rows, inverse, gain):
    weighted = grad_out * gain
    return inverse * (
        weighted
        - jnp.mean(weighted, axis=-1, keepdims=True)
        - unit_rows * jnp.mean(weighted * unit_rows, axis=-1, keepdims=True)
    )


def matmul(left_side, right_side):
    return jnp.einsum("npd,de->npe", left_side, right_side, preferred_element_type=F32)


def matmul_back(left_side, right_side):
    return jnp.einsum("npe,de->npd", left_side, right_side, preferred_element_type=F32)


def gelu_grad(pre_act, upstream):
    return jax.vjp(jax.nn.gelu, pre_act)[1](upstream)[0]


def slopes_for(first_head, head_total):
    return jnp.exp2(-8.0 * (first_head + jnp.arange(head_total) + 1).astype(F32) / HEADS)


def split_heads(values, head_count):
    return values.reshape(values.shape[0], values.shape[1], head_count, HEAD_DIM)


def attend_forward(query_rows, key_rows, value_rows, bias):
    head_count = bias.shape[1]
    scores = (
        jnp.einsum(
            "nqhd,nkhd->nhqk",
            split_heads(query_rows, head_count),
            split_heads(key_rows, head_count),
            preferred_element_type=F32,
        )
        * HEAD_DIM ** (-0.5)
        + bias
    )
    highest = jnp.max(scores, axis=-1, keepdims=True)
    shifted = jnp.exp(scores - highest)
    denominator = jnp.sum(shifted, axis=-1, keepdims=True)
    probabilities = (shifted / denominator).astype(BF16)
    mixed_heads = jnp.einsum(
        "nhqk,nkhd->nqhd", probabilities, split_heads(value_rows, head_count), preferred_element_type=F32
    )
    return (mixed_heads.reshape(query_rows.shape).astype(BF16), probabilities)


def attend_backward(query_rows, key_rows, value_rows, probabilities, grad_mixed):
    head_count = probabilities.shape[1]
    query_heads = split_heads(query_rows, head_count)
    key_heads = split_heads(key_rows, head_count)
    value_heads = split_heads(value_rows, head_count)
    grad_heads = split_heads(grad_mixed, head_count)
    scale_factor = HEAD_DIM ** (-0.5)
    grad_probs = jnp.einsum("nqhd,nkhd->nhqk", grad_heads, value_heads, preferred_element_type=F32)
    grad_values = jnp.einsum("nhqk,nqhd->nkhd", probabilities, grad_heads, preferred_element_type=F32)
    wide = probabilities.astype(F32)
    inner_sum = jnp.sum(grad_probs * wide, axis=-1, keepdims=True)
    grad_scores = (wide * (grad_probs - inner_sum)).astype(BF16)
    grad_queries = jnp.einsum("nhqk,nkhd->nqhd", grad_scores, key_heads, preferred_element_type=F32)
    grad_keys = jnp.einsum("nhqk,nqhd->nkhd", grad_scores, query_heads, preferred_element_type=F32)
    row_shape = query_rows.shape
    return (
        (grad_queries * scale_factor).reshape(row_shape).astype(BF16),
        (grad_keys * scale_factor).reshape(row_shape).astype(BF16),
        grad_values.reshape(row_shape).astype(BF16),
    )


def contrast(pooled, present):
    total = pooled.shape[1]
    inverse = lax.rsqrt(jnp.mean(pooled * pooled, axis=-1, keepdims=True) + 1e-06)
    unit = pooled * inverse
    scale = LOGIT_SCALE / pooled.shape[2]
    logits = jnp.dot(unit[0], unit[1].T, precision=lax.Precision.HIGHEST) * scale
    absent = 10000.0 * (1.0 - present)
    by_row = logits - absent[None, :]
    by_column = logits - absent[:, None]
    row_total = jax.nn.logsumexp(by_row, axis=1, keepdims=True)
    column_total = jax.nn.logsumexp(by_column, axis=0, keepdims=True)
    same = jnp.eye(total, dtype=F32)
    diagonal = jnp.sum(logits * same, axis=1)
    loss = jnp.sum(present * (row_total[:, 0] + column_total[0] - 2.0 * diagonal)) / (2.0 * total)
    grad_logits = (
        present[:, None] * jnp.exp(by_row - row_total)
        + present[None, :] * jnp.exp(by_column - column_total)
        - 2.0 * same * present[:, None]
    ) * (scale / (2.0 * total))
    grad_unit = jnp.stack(
        [
            jnp.dot(grad_logits, unit[1], precision=lax.Precision.HIGHEST),
            jnp.dot(grad_logits.T, unit[0], precision=lax.Precision.HIGHEST),
        ]
    )
    return loss, inverse * (grad_unit - unit * jnp.mean(grad_unit * unit, axis=-1, keepdims=True))


def flipped(array, axis, bit):
    return lax.ppermute(array, axis, [(i, i ^ (1 << bit)) for i in range(lax.axis_size(axis))])


def other_half(weight, quarter):
    rows = weight.shape[0] // 4
    mine = flipped(lax.dynamic_slice_in_dim(weight, quarter * rows, rows, 0), "mod", 0)
    beside = flipped(mine, "dp", 1)
    odd = quarter >= 2
    pair = jnp.stack([jnp.where(odd, beside, mine), jnp.where(odd, mine, beside)])
    swapped = flipped(pair, "dp", 0)
    odd = quarter % 2 == 1
    whole = jnp.stack([jnp.where(odd, swapped, pair), jnp.where(odd, pair, swapped)], axis=1)
    return whole.reshape(weight.shape)


def block_order(width, count):
    bits = count.bit_length() - 1
    block = width // count
    rows = jnp.arange(width)
    place = rows // block
    partner = jnp.zeros_like(place)
    for bit in range(bits):
        partner = partner | (((place >> (bits - 1 - bit)) & 1) << bit)
    source = (lax.axis_index("dp") ^ partner) * block + rows % block
    return (source[:, None] == jnp.arange(width)[None, :]).astype(BF16)


def ordered(order, values):
    flat = values.reshape(-1, values.shape[-1])
    return jnp.einsum("jd,rd->jr", order, flat, preferred_element_type=F32).astype(BF16)


def summed(left_rows, grad_rows):
    count = lax.axis_size("dp")
    flat = grad_rows.reshape(-1, grad_rows.shape[-1])
    half = left_rows.shape[0] // 2
    send = jnp.dot(left_rows[half:], flat, preferred_element_type=F32).astype(BF16)
    keep = jnp.dot(left_rows[:half], flat, preferred_element_type=F32).astype(BF16)
    bits = count.bit_length() - 1
    for bit in range(bits):
        got = flipped(send, "dp", bit)
        if bit == bits - 1:
            return keep.astype(F32) + got.astype(F32)
        half = half // 2
        send = (keep[half:].astype(F32) + got[half:].astype(F32)).astype(BF16)
        keep = (keep[:half].astype(F32) + got[:half].astype(F32)).astype(BF16)


def summed_blocks(blocks):
    bits = lax.axis_size("dp").bit_length() - 1
    for bit in range(bits):
        half = blocks.shape[0] // 2
        blocks = blocks[:half] + flipped(blocks[half:], "dp", bit)
    return blocks[0]


def shards(
    patch_tokens,
    grid_coords,
    has_radar,
    enc_gains,
    enc_project,
    enc_mixer,
    enc_expand,
    enc_reduce,
    cross_norms,
    cross_gain,
    cross_query,
    cross_keyval,
    cross_mixer,
    cross_expand,
    cross_reduce,
    enc_cotangent,
    joined_cotangent,
):
    item_count, patches, model_width = patch_tokens.shape[1:]
    half_index = lax.axis_index("mod")
    dp_index = lax.axis_index("dp")
    dp_size = lax.axis_size("dp")
    is_radar = half_index == 1
    quarter = dp_index & 3
    quarter = (quarter >> 1) * 2 + (quarter & 1)
    local_heads = cross_query.shape[1] // HEAD_DIM

    qkv_own = jnp.concatenate([cross_query, cross_keyval[0], cross_keyval[1]], axis=1)
    qkv_other = other_half(qkv_own, quarter)
    mixer_other = other_half(cross_mixer, quarter)
    expand_other = other_half(cross_expand, quarter)
    reduce_other = other_half(cross_reduce, quarter)
    order = block_order(model_width, dp_size)

    grid_rows = grid_coords[:, 0, :].astype(F32)
    grid_columns = grid_coords[:, 1, :].astype(F32)
    across = grid_rows[:, :, None] - grid_rows[:, None, :]
    upward = grid_columns[:, :, None] - grid_columns[:, None, :]
    distance = jnp.sqrt(across * across + upward * upward)

    def bias_of(first, count):
        return -slopes_for(first, count)[None, :, None, None] * distance[:, None]

    tokens = patch_tokens[0].astype(F32)
    gain_pair = enc_gains[0]
    normed, unit_one, inverse_one = norm_forward(tokens, gain_pair[0])
    normed = normed.astype(BF16)
    project = matmul(normed, enc_project[0]).astype(BF16)
    query_rows = project[..., :model_width]
    key_rows = project[..., model_width : 2 * model_width]
    value_rows = project[..., 2 * model_width :]
    mixed_heads, probs = attend_forward(query_rows, key_rows, value_rows, bias_of(0, HEADS))
    residual = tokens + matmul(mixed_heads, enc_mixer[0])
    normed_two, unit_two, inverse_two = norm_forward(residual, gain_pair[1])
    normed_two = normed_two.astype(BF16)
    expanded = matmul(normed_two, enc_expand[0])
    hidden = jax.nn.gelu(expanded).astype(BF16)
    encoded = (residual + matmul(hidden, enc_reduce[0])).astype(BF16)
    partner = flipped(encoded, "mod", 0)

    present_row = jnp.broadcast_to(has_radar.astype(F32)[:, None], (item_count, 128))
    pooled_own = jnp.concatenate([jnp.mean(encoded.astype(F32), axis=1), present_row], axis=1)
    gathered = lax.all_gather(pooled_own, ("mod", "dp"), axis=0, tiled=True)
    total_items = gathered.shape[0] // 2
    gathered = gathered.reshape(2, total_items, model_width + 128)
    loss_value, pool_grad = contrast(gathered[:, :, :model_width], gathered[0, :, model_width])
    own_pool_grad = lax.dynamic_slice(
        pool_grad, (half_index, dp_index * item_count, 0), (1, item_count, model_width)
    )[0]

    radar_tokens = jnp.where(is_radar, encoded, partner).astype(F32)
    optical = jnp.where(is_radar, partner, encoded).astype(F32)
    query_in, unit_query, inverse_query = norm_forward(radar_tokens, cross_norms[1])
    keyval_in, unit_keyval, inverse_keyval = norm_forward(optical, cross_norms[0])
    query_in = query_in.astype(BF16)
    keyval_in = keyval_in.astype(BF16)
    width = local_heads * HEAD_DIM
    parts = []
    for qkv, mixer, first in (
        (qkv_own, cross_mixer, half_index * local_heads),
        (qkv_other, mixer_other, (1 - half_index) * local_heads),
    ):
        queries = matmul(query_in, qkv[:, :width]).astype(BF16)
        keyvals = matmul(keyval_in, qkv[:, width:]).astype(BF16)
        keys, values = keyvals[..., :width], keyvals[..., width:]
        mixed, cross_probs = attend_forward(queries, keys, values, bias_of(first, local_heads))
        parts.append((qkv, mixer, queries, keys, values, mixed, cross_probs))
    cross_resid = radar_tokens + matmul(parts[0][5], cross_mixer) + matmul(parts[1][5], mixer_other)
    cross_normed, unit_cross, inverse_cross = norm_forward(cross_resid, cross_gain)
    cross_normed = cross_normed.astype(BF16)
    wide_own = matmul(cross_normed, cross_expand)
    wide_other = matmul(cross_normed, expand_other)
    hidden_own = jax.nn.gelu(wide_own).astype(BF16)
    hidden_other = jax.nn.gelu(wide_other).astype(BF16)
    present = has_radar.astype(F32)[:, None, None]

    def own_image(values):
        return lax.dynamic_slice_in_dim(values, half_index, 1, 0)

    joined_mine = own_image(present) * (
        own_image(cross_resid)
        + matmul(own_image(hidden_own), cross_reduce)
        + matmul(own_image(hidden_other), reduce_other)
    )
    joined_mine = joined_mine.astype(BF16)
    joined_theirs = flipped(joined_mine, "mod", 0)
    joined_tokens = jnp.concatenate(
        [jnp.where(is_radar, joined_theirs, joined_mine), jnp.where(is_radar, joined_mine, joined_theirs)]
    )

    grad_joined = present * joined_cotangent.astype(F32)
    grad_branch = grad_joined.astype(BF16)
    creduce_sum = summed(ordered(order, grad_branch), hidden_own)
    gexp_own = gelu_grad(wide_own, matmul_back(grad_branch, cross_reduce)).astype(BF16)
    gexp_other = gelu_grad(wide_other, matmul_back(grad_branch, reduce_other)).astype(BF16)
    cexpand_sum = summed(ordered(order, cross_normed), gexp_own)
    grad_cnormed = matmul_back(gexp_own, cross_expand) + matmul_back(gexp_other, expand_other)
    gain_grad = jnp.sum(own_image(grad_cnormed * unit_cross), axis=(0, 1))
    grad_cresid = grad_joined + norm_backward(grad_cnormed, unit_cross, inverse_cross, cross_gain)
    grad_attention = grad_cresid.astype(BF16)
    cmixer_sum = summed(ordered(order, grad_attention), parts[0][5])
    grad_q, grad_kv = [], []
    for qkv, mixer, queries, keys, values, mixed, cross_probs in parts:
        grad_cmixed = matmul_back(grad_attention, mixer).astype(BF16)
        gq, gk, gv = attend_backward(queries, keys, values, cross_probs, grad_cmixed)
        grad_q.append(gq)
        grad_kv.append(jnp.concatenate([gk, gv], axis=-1))
    query_sum = summed(ordered(order, query_in), grad_q[0])
    keyval_sum = summed(ordered(order, keyval_in), grad_kv[0])
    grad_query_in = matmul_back(grad_q[0], qkv_own[:, :width]) + matmul_back(grad_q[1], qkv_other[:, :width])
    grad_keyval_in = matmul_back(grad_kv[0], qkv_own[:, width:]) + matmul_back(grad_kv[1], qkv_other[:, width:])
    own_norm_in = jnp.where(is_radar, grad_query_in, grad_keyval_in)
    own_unit = jnp.where(is_radar, unit_query, unit_keyval)
    own_inverse = jnp.where(is_radar, inverse_query, inverse_keyval)
    own_gain = jnp.where(is_radar, cross_norms[1], cross_norms[0])
    norms_grad = jnp.sum(own_norm_in * own_unit, axis=(0, 1))
    grad_own_norm = norm_backward(own_norm_in, own_unit, own_inverse, own_gain)
    grad_out = (
        enc_cotangent[0].astype(F32)
        + own_pool_grad[:, None, :] / patches
        + grad_own_norm
        + jnp.where(is_radar, grad_cresid, 0.0)
    )

    grad_narrow = grad_out.astype(BF16)
    reduce_sum = summed(ordered(order, grad_narrow), hidden)
    grad_hidden = matmul_back(grad_narrow, enc_reduce[0])
    grad_expanded = gelu_grad(expanded, grad_hidden).astype(BF16)
    expand_sum = summed(ordered(order, normed_two), grad_expanded)
    grad_normed_two = matmul_back(grad_expanded, enc_expand[0])
    gain_two = jnp.sum(grad_normed_two * unit_two, axis=(0, 1))
    grad_resid = grad_out + norm_backward(grad_normed_two, unit_two, inverse_two, gain_pair[1])
    grad_mixer_out = grad_resid.astype(BF16)
    mixer_sum = summed(ordered(order, mixed_heads), grad_mixer_out)
    grad_mixed = matmul_back(grad_mixer_out, enc_mixer[0]).astype(BF16)
    grad_project = jnp.concatenate(
        attend_backward(query_rows, key_rows, value_rows, probs, grad_mixed), axis=-1
    )
    project_sum = summed(ordered(order, normed), grad_project)
    grad_normed = matmul_back(grad_project, enc_project[0])
    gain_one = jnp.sum(grad_normed * unit_one, axis=(0, 1))
    patch_grad = grad_resid + norm_backward(grad_normed, unit_one, inverse_one, gain_pair[0])

    vectors = jnp.stack([gain_one, gain_two, norms_grad, gain_grad])
    placed = jnp.dot(vectors, order.astype(F32).T, precision=lax.Precision.HIGHEST)
    block = model_width // dp_size
    vector_sum = summed_blocks(jnp.moveaxis(placed.reshape(4, dp_size, block), 1, 0))
    gain_sum = vector_sum[3] + flipped(vector_sum[3], "mod", 0)
    return (
        encoded[None],
        joined_tokens,
        loss_value,
        patch_grad[None],
        vector_sum[None, :2],
        project_sum[None],
        mixer_sum[None],
        expand_sum[None],
        reduce_sum.T[None],
        vector_sum[2:3],
        gain_sum,
        query_sum,
        jnp.stack([keyval_sum[:, :width], keyval_sum[:, width:]]),
        cmixer_sum.T,
        cexpand_sum,
        creduce_sum.T,
    )


def solution(mesh):
    placed = (
        P("mod", "dp", None, None),
        P("dp", None, None),
        P("dp"),
        P("mod", None, None),
        P("mod", None, None),
        P("mod", None, None),
        P("mod", None, None),
        P("mod", None, None),
        P(),
        P(),
        P(None, "mod"),
        P(None, None, "mod"),
        P("mod", None),
        P(None, "mod"),
        P("mod", None),
        P("mod", "dp", None, None),
        P("dp", None, None),
    )
    return jax.shard_map(
        shards,
        mesh=mesh,
        in_specs=placed,
        out_specs=(
            P("mod", "dp", None, None),
            P("dp", None, None),
            P(),
            P("mod", "dp", None, None),
            P("mod", None, "dp"),
            P("mod", "dp", None),
            P("mod", "dp", None),
            P("mod", "dp", None),
            P("mod", None, "dp"),
            P("mod", "dp"),
            P("dp"),
            P("dp", "mod"),
            P(None, "dp", "mod"),
            P("mod", "dp"),
            P("dp", "mod"),
            P("mod", "dp"),
        ),
        check_vma=False,
    )
```

time: 1260 us -> 615 us (0.49)
  waiting for transfers between devices: 839 us -> 168 us
  blocking collectives: 127 us -> 66.8 us
  starting transfers between devices: 4.62 us -> 36.8 us
  matrix products: 130 us -> 159 us
  other arithmetic: 50 us -> 77.8 us
  local copies, waits for them, and re-layouts: 78.6 us -> 92.4 us
  between operations: 18.1 us -> 5.31 us
    reduce_scatter x8 -> x0, waiting for transfers between devices: 624 us -> none  [the longest x1 116 us: shards(): lax.psum_scatter(every_front[3], 'dp', scatter_dimension=0, tiled=True)]
    unnamed x16 -> x0, waiting for transfers between devices: 164 us -> none
    ppermute x2 -> x55, waiting for transfers between devices: 18.1 us -> 168 us  [flipped(): lax.ppermute(array, axis, [(i, i ^ 1 << bit) for i in range(lax.axis_size...]
    unnamed x2 -> x0, blocking collectives: 83.8 us -> none
    ppermute x2 -> x55, starting transfers between devices: 3.33 us -> 36.8 us  [flipped(): lax.ppermute(array, axis, [(i, i ^ 1 << bit) for i in range(lax.axis_size...]
    psum x2 -> x0, waiting for transfers between devices: 33 us -> none  [the longest x1 33 us: shards(): lax.psum(matmul(cross_hidden, cross_reduce).astype(jnp.bfloat16), 'mod')]
    convert_element_type x4 -> x44, other arithmetic: 5.73 us -> 33.3 us  [the longest x3 8.09 us: attend_forward(): probabilities = (shifted / denominator).astype(BF16)]
    all_gather x1, blocking collectives: 42.9 us -> 66.8 us  [shards(): gathered = lax.all_gather(pooled_own, ('mod', 'dp'), axis=0, tiled=True)]
  transfers between devices with their start and end apart: 15 -> 55, of which waited for: 11 -> 30; matrix products, arithmetic and copies ran while one was open for 10% -> 50% of each run, Pallas kernels for 0% -> 0%
where the time goes in v1:
time: 615 us; the launch traced here: 606 us
  waiting for transfers between devices  168 us (27%)
  matrix products  159 us (26%)
  local copies, waits for them, and re-layouts  92.4 us (15%)
  other arithmetic  77.8 us (13%)
  blocking collectives  66.8 us (11%)
  starting transfers between devices  36.8 us (6%)
    ppermute x55, waiting for transfers between devices, flipped(): lax.ppermute(array, axis, [(i, i ^ 1 << bit) for i in range(lax.axis_size...  168 us
    all_gather x1, blocking collectives, shards(): gathered = lax.all_gather(pooled_own, ('mod', 'dp'), axis=0, tiled=True)  66.8 us
    dot_general x13, matrix products, matmul_back(): jnp.einsum('npe,de->npd', left_side, right_side, preferred_element_type=F32)  42.4 us
    ppermute x55, starting transfers between devices, flipped(): lax.ppermute(array, axis, [(i, i ^ 1 << bit) for i in range(lax.axis_size...  36.8 us
    dot_general x14, matrix products, matmul(): jnp.einsum('npd,de->npe', left_side, right_side, preferred_element_type=F32)  28.9 us
    unnamed x382, local copies, waits for them, and re-layouts  24.1 us
    sub x3, matrix products, attend_forward(): shifted = jnp.exp(scores - highest)  16.5 us
    dot_general x9, matrix products, ordered(): jnp.einsum('jd,rd->jr', order, flat, preferred_element_type=F32)  15.3 us
  transfers between devices with their start and end apart: 55, of which 30 were waited for; matrix products, arithmetic and copies ran while one was open for 50% of the time, Pallas kernels for 0%

profile of v1, /device:TPU:0, one launch (start us, length us, event | category | flops | bytes accessed | tf_op | source)
XLA Modules:
  0.0 606.0 jit_solution(11889328109605807254)
XLA Ops:
  27.9 7.2 %fusion.244 = (f32[2,12,256]{2,1,0:T(8,128)}, f32[2,12,256,256]{2,3,1,0:T(8,128)}) fusion(f32[2,256,256]{1,2,0:T(8,128)} %add_sqrt_fusion, f32[12]{0:T(128)} %exponential_negate_fusion.2, bf16[2,256,12,64]{1,3,2,0:T(8,128)(2,1)} %bitcast.472, bf16[2,256,12,64]{1,3,2,0:T(8,128)(2,1)} %bitcast.470), kind=kOutput, calls=%fused_computation.510 | convolution fusion | flops 209191168 | bytes 8413232 | tf_op jit(solution)/shard_map/sub | solution.py:62
  44.5 5.9 multiply_convert_fusion
  83.2 66.8 %all-gather = f32[32,2,896]{2,1,0:T(2,128)} all-gather(f32[1,2,896]{2,1,0:T(2,128)S(1)} %maximum_bitcast_fusion.3), channel_id=1, replica_groups=mesh['mod'=2,'dp'=16] {'mod','dp'}, dimensions={0}, use_global_device_ids=true | all-gather | bytes 236544 | tf_op jit(solution)/shard_map/all_gather | solution.py:241
  174.1 4.3 fusion.247
  208.3 5.0 fusion.246
  246.7 4.3 add_multiply_fusion
  251.0 9.9 %multiply_reduce_fusion.10 = (f32[2,256]{1,0:T(2,128)}, f32[2,256]{1,0:T(2,128)}, f32[2,256,768]{2,1,0:T(8,128)}) fusion(f32[768]{0:T(1024)} %param.26, f32[2,256,768]{2,1,0:T(8,128)} %get-tuple-element.44, f32[2,256,768]{2,1,0:T(8,128)} %fusion.53, bf16[768,1536,1]{1,0,2:T(8,128)(2,1)} %bitcast.486, f32[2,256,1536]{2,1,0:T(8,128)} %get-tuple-element.141, ...), kind=kOutput, calls=%fused_computation.205 | convolution fusion | flops 2433612800 | bytes 13376512 | tf_op jit(solution)/shard_map/npe,de->npd/dot_general | solution.py:34
  311.2 9.2 %fusion.11 = bf16[2,256,3072]{2,1,0:T(8,128)(2,1)S(1)} fusion(f32[2,256,3072]{2,1,0:T(8,128)} %get-tuple-element.133, bf16[2,256,768]{2,1,0:T(8,128)(2,1)S(1)} %get-tuple-element.38, bf16[1,3072,768]{2,1,0:T(8,128)(2,1)} %param.24), kind=kOutput, calls=%fused_computation.15 | convolution fusion | flops 2447376384 | bytes 14942208 | tf_op jit(solution)/shard_map/npe,de->npd/dot_general | solution.py:34
  335.2 5.5 fusion.3
  340.8 4.3 fusion.4
  381.9 5.2 fusion.97
  404.6 4.1 collective-permute-done.17
  421.1 5.0 collective-permute-done.36
  426.1 4.3 collective-permute-done.45
  430.4 4.4 collective-permute-done.37
  434.8 5.0 collective-permute-done.46
  440.5 4.2 collective-permute-done.38
  451.7 4.6 collective-permute-done.40
  456.9 5.7 collective-permute-done.23
  462.8 4.9 collective-permute-done.41
  468.0 4.9 collective-permute-done.24
  472.9 7.1 %collective-permute-done.42 = bf16[48,768]{1,0:T(8,128)(2,1)S(1)} collective-permute-done((bf16[48,768]{1,0:T(8,128)(2,1)S(1)}, bf16[48,768]{1,0:T(8,128)(2,1)S(1)}, u32[]{:S(2)}, u32[]{:S(2)}) %collective-permute-start.42) | collective-permute-done | bytes 73760 | tf_op jit(solution)/shard_map/ppermute | solution.py:122
  480.1 5.3 collective-permute-done.25
  487.5 7.9 %collective-permute-done.52 = bf16[192,1536]{1,0:T(8,128)(2,1)S(1)} collective-permute-done((bf16[192,1536]{1,0:T(8,128)(2,1)S(1)}, bf16[192,1536]{1,0:T(8,128)(2,1)S(1)}, u32[]{:S(2)}, u32[]{:S(2)}) %collective-permute-start.52) | collective-permute-done | bytes 589856 | tf_op jit(solution)/shard_map/ppermute | solution.py:122
  497.9 4.4 collective-permute-done.53
  504.3 5.2 collective-permute-done.50
  511.8 9.3 %collective-permute-done.19 = bf16[192,2304]{1,0:T(8,128)(2,1)S(1)} collective-permute-done((bf16[192,2304]{1,0:T(8,128)(2,1)S(1)}, bf16[192,2304]{1,0:T(8,128)(2,1)S(1)}, u32[]{:S(2)}, u32[]{:S(2)}) %collective-permute-start.19) | collective-permute-done | bytes 884768 | tf_op jit(solution)/shard_map/ppermute | solution.py:122
  524.3 7.3 %collective-permute-done.20 = bf16[96,2304]{1,0:T(8,128)(2,1)S(1)} collective-permute-done((bf16[96,2304]{1,0:T(8,128)(2,1)S(1)}, bf16[96,2304]{1,0:T(8,128)(2,1)S(1)}, u32[]{:S(2)}, u32[]{:S(2)}) %collective-permute-start.20) | collective-permute-done | bytes 442400 | tf_op jit(solution)/shard_map/ppermute | solution.py:122
  541.1 10.4 %collective-permute-done.27 = bf16[192,3072]{1,0:T(8,128)(2,1)S(1)} collective-permute-done((bf16[192,3072]{1,0:T(8,128)(2,1)S(1)}, bf16[192,3072]{1,0:T(8,128)(2,1)S(1)}, u32[]{:S(2)}, u32[]{:S(2)}) %collective-permute-start.27) | collective-permute-done | bytes 1179680 | tf_op jit(solution)/shard_map/ppermute | solution.py:122
  553.8 18.0 %collective-permute-done.31 = bf16[192,3072]{1,0:T(8,128)(2,1)S(1)} collective-permute-done((bf16[192,3072]{1,0:T(8,128)(2,1)S(1)}, bf16[192,3072]{1,0:T(8,128)(2,1)S(1)}, u32[]{:S(2)}, u32[]{:S(2)}) %collective-permute-start.31) | collective-permute-done | bytes 1179680 | tf_op jit(solution)/shard_map/ppermute | solution.py:122
  576.5 12.5 %collective-permute-done.32 = bf16[96,3072]{1,0:T(8,128)(2,1)S(1)} collective-permute-done((bf16[96,3072]{1,0:T(8,128)(2,1)S(1)}, bf16[96,3072]{1,0:T(8,128)(2,1)S(1)}, u32[]{:S(2)}, u32[]{:S(2)}) %collective-permute-start.32) | collective-permute-done | bytes 589856 | tf_op jit(solution)/shard_map/ppermute | solution.py:122
  591.1 12.5 %collective-permute-done.33 = bf16[48,3072]{1,0:T(8,128)(2,1)S(1)} collective-permute-done((bf16[48,3072]{1,0:T(8,128)(2,1)S(1)}, bf16[48,3072]{1,0:T(8,128)(2,1)S(1)}, u32[]{:S(2)}, u32[]{:S(2)}) %collective-permute-start.33) | collective-permute-done | bytes 294944 | tf_op jit(solution)/shard_map/ppermute | solution.py:122
  (725 shorter events, 326.1 us)
Async XLA Ops:
  2.4 65.3 %collective-permute-start.4 = (bf16[96,768]{1,0:T(8,128)(2,1)}, bf16[96,768]{1,0:T(8,128)(2,1)}, u32[]{:S(2)}, u32[]{:S(2)}) collective-permute-start(bf16[96,768]{1,0:T(8,128)(2,1)} %constant_dynamic-slice_fusion.2), channel_id=1, source_target_pairs={{0,16},{16,0},{1,17},{17,1},{2,18},{18,2},{3,19},{19,3},{4,20},{20... | collective-permute-start | bytes 442376 | tf_op jit(solution)/shard_map/ppermute | solution.py:122
  7.3 70.6 %collective-permute-start.7 = (bf16[192,1536]{1,0:T(8,128)(2,1)}, bf16[192,1536]{1,0:T(8,128)(2,1)}, u32[]{:S(2)}, u32[]{:S(2)}) collective-permute-start(bf16[192,1536]{1,0:T(8,128)(2,1)} %constant_dynamic-slice_fusion.1), channel_id=1, source_target_pairs={{0,16},{16,0},{1,17},{17,1},{2,18},{18,2},{3,19},{19,3},{4,20},{20... | collective-permute-start | bytes 1769480 | tf_op jit(solution)/shard_map/ppermute | solution.py:122
  9.3 69.2 %collective-permute-start.10 = (bf16[384,768]{1,0:T(8,128)(2,1)}, bf16[384,768]{1,0:T(8,128)(2,1)}, u32[]{:S(2)}, u32[]{:S(2)}) collective-permute-start(bf16[384,768]{1,0:T(8,128)(2,1)} %constant_dynamic-slice_fusion), channel_id=1, source_target_pairs={{0,16},{16,0},{1,17},{17,1},{2,18},{18,2},{3,19},{19,3},{4,20},{20... | collective-permute-start | bytes 1769480 | tf_op jit(solution)/shard_map/ppermute | solution.py:122
  13.5 61.9 %collective-permute-start.1 = (bf16[192,1152]{1,0:T(8,128)(2,1)}, bf16[192,1152]{1,0:T(8,128)(2,1)}, u32[]{:S(2)}, u32[]{:S(2)}) collective-permute-start(bf16[192,1152]{1,0:T(8,128)(2,1)} %fusion.173), channel_id=1, source_target_pairs={{0,16},{16,0},{1,17},{17,1},{2,18},{18,2},{3,19},{19,3},{4,20},{20... | collective-permute-start | bytes 1327112 | tf_op jit(solution)/shard_map/ppermute | solution.py:122
  53.9 26.0 %collective-permute-start = (bf16[2,256,768]{2,1,0:T(8,128)(2,1)}, bf16[2,256,768]{2,1,0:T(8,128)(2,1)}, u32[]{:S(2)}, u32[]{:S(2)}) collective-permute-start(bf16[2,256,768]{2,1,0:T(8,128)(2,1)} %add_convert_fusion.6), channel_id=1, source_target_pairs={{0,16},{16,0},{1,17},{17,1},{2,18},{18,2},{3,19},{19,3},{4,20},{20... | collective-permute-start | bytes 2359304 | tf_op jit(solution)/shard_map/ppermute | solution.py:122
  75.5 112.2 %collective-permute-start.2 = (bf16[192,1152]{1,0:T(8,128)(2,1)}, bf16[192,1152]{1,0:T(8,128)(2,1)}, u32[]{:S(2)}, u32[]{:S(2)}) collective-permute-start(bf16[192,1152]{1,0:T(8,128)(2,1)} %collective-permute-done.1), channel_id=1, source_target_pairs={{0,2},{1,3},{2,0},{3,1},{4,6},{5,7},{6,4},{7,5},{8,10},{9,11},{10,... | collective-permute-start | bytes 1327112 | tf_op jit(solution)/shard_map/ppermute | solution.py:122
  77.9 111.4 %collective-permute-start.8 = (bf16[192,1536]{1,0:T(8,128)(2,1)}, bf16[192,1536]{1,0:T(8,128)(2,1)}, u32[]{:S(2)}, u32[]{:S(2)}) collective-permute-start(bf16[192,1536]{1,0:T(8,128)(2,1)} %collective-permute-done.7), channel_id=1, source_target_pairs={{0,2},{1,3},{2,0},{3,1},{4,6},{5,7},{6,4},{7,5},{8,10},{9,11},{10,... | collective-permute-start | bytes 1769480 | tf_op jit(solution)/shard_map/ppermute | solution.py:122
  78.5 113.6 %collective-permute-start.11 = (bf16[384,768]{1,0:T(8,128)(2,1)}, bf16[384,768]{1,0:T(8,128)(2,1)}, u32[]{:S(2)}, u32[]{:S(2)}) collective-permute-start(bf16[384,768]{1,0:T(8,128)(2,1)} %collective-permute-done.10), channel_id=1, source_target_pairs={{0,2},{1,3},{2,0},{3,1},{4,6},{5,7},{6,4},{7,5},{8,10},{9,11},{10,... | collective-permute-start | bytes 1769480 | tf_op jit(solution)/shard_map/ppermute | solution.py:122
  192.0 48.2 %collective-permute-start.9 = (bf16[2,192,1536]{2,1,0:T(8,128)(2,1)}, bf16[2,192,1536]{2,1,0:T(8,128)(2,1)}, u32[]{:S(2)}, u32[]{:S(2)}) collective-permute-start(bf16[2,192,1536]{2,1,0:T(8,128)(2,1)} %pad_maximum_fusion.3), channel_id=1, source_target_pairs={{0,1},{1,0},{2,3},{3,2},{4,5},{5,4},{6,7},{7,6},{8,9},{9,8},{10,11... | collective-permute-start | bytes 3538952 | tf_op jit(solution)/shard_map/ppermute | solution.py:122
  195.4 46.6 %collective-permute-start.12 = (bf16[2,384,768]{2,1,0:T(8,128)(2,1)}, bf16[2,384,768]{2,1,0:T(8,128)(2,1)}, u32[]{:S(2)}, u32[]{:S(2)}) collective-permute-start(bf16[2,384,768]{2,1,0:T(8,128)(2,1)} %pad_maximum_fusion.4), channel_id=1, source_target_pairs={{0,1},{1,0},{2,3},{3,2},{4,5},{5,4},{6,7},{7,6},{8,9},{9,8},{10,11... | collective-permute-start | bytes 3538952 | tf_op jit(solution)/shard_map/ppermute | solution.py:122
  237.9 208.5 %collective-permute-start.47 = (bf16[384,1536]{1,0:T(8,128)(2,1)}, bf16[384,1536]{1,0:T(8,128)(2,1)}, u32[]{:S(2)}, u32[]{:S(2)}) collective-permute-start(bf16[384,1536]{1,0:T(8,128)(2,1)} %convolution_convert_fusion.9), channel_id=1, source_target_pairs={{0,1},{1,0},{2,3},{3,2},{4,5},{5,4},{6,7},{7,6},{8,9},{9,8},{10,11... | collective-permute-start | bytes 3538952 | tf_op jit(solution)/shard_map/ppermute | solution.py:122
  238.0 210.5 %collective-permute-start.51 = (bf16[384,1536]{1,0:T(8,128)(2,1)}, bf16[384,1536]{1,0:T(8,128)(2,1)}, u32[]{:S(2)}, u32[]{:S(2)}) collective-permute-start(bf16[384,1536]{1,0:T(8,128)(2,1)} %convolution_convert_fusion.7), channel_id=1, source_target_pairs={{0,1},{1,0},{2,3},{3,2},{4,5},{5,4},{6,7},{7,6},{8,9},{9,8},{10,11... | collective-permute-start | bytes 3538952 | tf_op jit(solution)/shard_map/ppermute | solution.py:122
  372.3 42.3 %collective-permute-start.13 = (bf16[1,256,768]{2,1,0:T(8,128)(2,1)}, bf16[1,256,768]{2,1,0:T(8,128)(2,1)}, u32[]{:S(2)}, u32[]{:S(2)}) collective-permute-start(bf16[1,256,768]{2,1,0:T(8,128)(2,1)} %fusion.148), channel_id=1, source_target_pairs={{0,16},{16,0},{1,17},{17,1},{2,18},{18,2},{3,19},{19,3},{4,20},{20... | collective-permute-start | bytes 1179656 | tf_op jit(solution)/shard_map/ppermute | solution.py:122
  401.0 12.3 %collective-permute-start.43 = (bf16[384,384]{1,0:T(8,128)(2,1)S(1)}, bf16[384,384]{1,0:T(8,128)(2,1)S(1)}, u32[]{:S(2)}, u32[]{:S(2)}) collective-permute-start(bf16[384,384]{1,0:T(8,128)(2,1)S(1)} %convolution_convert_fusion.28), channel_id=1, source_target_pairs={{0,1},{1,0},{2,3},{3,2},{4,5},{5,4},{6,7},{7,6},{8,9},{9,8},{10,11... | collective-permute-start | bytes 884744 | tf_op jit(solution)/shard_map/ppermute | solution.py:122
  413.3 32.1 %collective-permute-start.39 = (bf16[384,768]{1,0:T(8,128)(2,1)S(1)}, bf16[384,768]{1,0:T(8,128)(2,1)S(1)}, u32[]{:S(2)}, u32[]{:S(2)}) collective-permute-start(bf16[384,768]{1,0:T(8,128)(2,1)S(1)} %copy-done.164), channel_id=1, source_target_pairs={{0,1},{1,0},{2,3},{3,2},{4,5},{5,4},{6,7},{7,6},{8,9},{9,8},{10,11... | collective-permute-start | bytes 1769480 | tf_op jit(solution)/shard_map/ppermute | solution.py:122
  414.3 31.8 %collective-permute-start.22 = (bf16[384,768]{1,0:T(8,128)(2,1)S(1)}, bf16[384,768]{1,0:T(8,128)(2,1)S(1)}, u32[]{:S(2)}, u32[]{:S(2)}) collective-permute-start(bf16[384,768]{1,0:T(8,128)(2,1)S(1)} %copy-done.165), channel_id=1, source_target_pairs={{0,1},{1,0},{2,3},{3,2},{4,5},{5,4},{6,7},{7,6},{8,9},{9,8},{10,11... | collective-permute-start | bytes 1769480 | tf_op jit(solution)/shard_map/ppermute | solution.py:122
  444.7 57.7 %collective-permute-start.18 = (bf16[384,2304]{1,0:T(8,128)(2,1)S(1)}, bf16[384,2304]{1,0:T(8,128)(2,1)S(1)}, u32[]{:S(2)}, u32[]{:S(2)}) collective-permute-start(bf16[384,2304]{1,0:T(8,128)(2,1)S(1)} %copy-done.161), channel_id=1, source_target_pairs={{0,1},{1,0},{2,3},{3,2},{4,5},{5,4},{6,7},{7,6},{8,9},{9,8},{10,11... | collective-permute-start | bytes 5308424 | tf_op jit(solution)/shard_map/ppermute | solution.py:122
  445.4 76.2 %collective-permute-start.26 = (bf16[384,3072]{1,0:T(8,128)(2,1)S(1)}, bf16[384,3072]{1,0:T(8,128)(2,1)S(1)}, u32[]{:S(2)}, u32[]{:S(2)}) collective-permute-start(bf16[384,3072]{1,0:T(8,128)(2,1)S(1)} %copy-done.160), channel_id=1, source_target_pairs={{0,1},{1,0},{2,3},{3,2},{4,5},{5,4},{6,7},{7,6},{8,9},{9,8},{10,11... | collective-permute-start | bytes 7077896 | tf_op jit(solution)/shard_map/ppermute | solution.py:122
  446.1 88.9 %collective-permute-start.30 = (bf16[384,3072]{1,0:T(8,128)(2,1)S(1)}, bf16[384,3072]{1,0:T(8,128)(2,1)S(1)}, u32[]{:S(2)}, u32[]{:S(2)}) collective-permute-start(bf16[384,3072]{1,0:T(8,128)(2,1)S(1)} %copy-done.159), channel_id=1, source_target_pairs={{0,1},{1,0},{2,3},{3,2},{4,5},{5,4},{6,7},{7,6},{8,9},{9,8},{10,11... | collective-permute-start | bytes 7077896 | tf_op jit(solution)/shard_map/ppermute | solution.py:122
  448.6 14.0 %collective-permute-start.23 = (bf16[192,768]{1,0:T(8,128)(2,1)S(1)}, bf16[192,768]{1,0:T(8,128)(2,1)S(1)}, u32[]{:S(2)}, u32[]{:S(2)}) collective-permute-start(bf16[192,768]{1,0:T(8,128)(2,1)S(1)} %get-tuple-element.83), channel_id=1, source_target_pairs={{0,2},{1,3},{2,0},{3,1},{4,6},{5,7},{6,4},{7,5},{8,10},{9,11},{10,... | collective-permute-start | bytes 884744 | tf_op jit(solution)/shard_map/ppermute | solution.py:122
  456.3 30.9 %collective-permute-start.48 = (bf16[192,1536]{1,0:T(8,128)(2,1)S(1)}, bf16[192,1536]{1,0:T(8,128)(2,1)S(1)}, u32[]{:S(2)}, u32[]{:S(2)}) collective-permute-start(bf16[192,1536]{1,0:T(8,128)(2,1)S(1)} %get-tuple-element.58), channel_id=1, source_target_pairs={{0,2},{1,3},{2,0},{3,1},{4,6},{5,7},{6,4},{7,5},{8,10},{9,11},{10,... | collective-permute-start | bytes 1769480 | tf_op jit(solution)/shard_map/ppermute | solution.py:122
  485.4 10.0 %collective-permute-start.52 = (bf16[192,1536]{1,0:T(8,128)(2,1)S(1)}, bf16[192,1536]{1,0:T(8,128)(2,1)S(1)}, u32[]{:S(2)}, u32[]{:S(2)}) collective-permute-start(bf16[192,1536]{1,0:T(8,128)(2,1)S(1)} %get-tuple-element.56), channel_id=1, source_target_pairs={{0,2},{1,3},{2,0},{3,1},{4,6},{5,7},{6,4},{7,5},{8,10},{9,11},{10,... | collective-permute-start | bytes 1769480 | tf_op jit(solution)/shard_map/ppermute | solution.py:122
  487.4 10.5 %collective-permute-start.49 = (bf16[96,1536]{1,0:T(8,128)(2,1)S(1)}, bf16[96,1536]{1,0:T(8,128)(2,1)S(1)}, u32[]{:S(2)}, u32[]{:S(2)}) collective-permute-start(bf16[96,1536]{1,0:T(8,128)(2,1)S(1)} %get-tuple-element.79), channel_id=1, source_target_pairs={{0,4},{1,5},{2,6},{3,7},{4,0},{5,1},{6,2},{7,3},{8,12},{9,13},{10,... | collective-permute-start | bytes 884744 | tf_op jit(solution)/shard_map/ppermute | solution.py:122
  497.9 11.6 %collective-permute-start.50 = (bf16[48,1536]{1,0:T(8,128)(2,1)S(1)}, bf16[48,1536]{1,0:T(8,128)(2,1)S(1)}, u32[]{:S(2)}, u32[]{:S(2)}) collective-permute-start(bf16[48,1536]{1,0:T(8,128)(2,1)S(1)} %add_convert_fusion.33), channel_id=1, source_target_pairs={{0,8},{1,9},{2,10},{3,11},{4,12},{5,13},{6,14},{7,15},{8,0},{9,1},... | collective-permute-start | bytes 442376 | tf_op jit(solution)/shard_map/ppermute | solution.py:122
  502.9 18.3 %collective-permute-start.19 = (bf16[192,2304]{1,0:T(8,128)(2,1)S(1)}, bf16[192,2304]{1,0:T(8,128)(2,1)S(1)}, u32[]{:S(2)}, u32[]{:S(2)}) collective-permute-start(bf16[192,2304]{1,0:T(8,128)(2,1)S(1)} %get-tuple-element.54), channel_id=1, source_target_pairs={{0,2},{1,3},{2,0},{3,1},{4,6},{5,7},{6,4},{7,5},{8,10},{9,11},{10,... | collective-permute-start | bytes 2654216 | tf_op jit(solution)/shard_map/ppermute | solution.py:122
  521.4 10.2 %collective-permute-start.20 = (bf16[96,2304]{1,0:T(8,128)(2,1)S(1)}, bf16[96,2304]{1,0:T(8,128)(2,1)S(1)}, u32[]{:S(2)}, u32[]{:S(2)}) collective-permute-start(bf16[96,2304]{1,0:T(8,128)(2,1)S(1)} %get-tuple-element.71), channel_id=1, source_target_pairs={{0,4},{1,5},{2,6},{3,7},{4,0},{5,1},{6,2},{7,3},{8,12},{9,13},{10,... | collective-permute-start | bytes 1327112 | tf_op jit(solution)/shard_map/ppermute | solution.py:122
  522.5 29.0 %collective-permute-start.27 = (bf16[192,3072]{1,0:T(8,128)(2,1)S(1)}, bf16[192,3072]{1,0:T(8,128)(2,1)S(1)}, u32[]{:S(2)}, u32[]{:S(2)}) collective-permute-start(bf16[192,3072]{1,0:T(8,128)(2,1)S(1)} %get-tuple-element.52), channel_id=1, source_target_pairs={{0,2},{1,3},{2,0},{3,1},{4,6},{5,7},{6,4},{7,5},{8,10},{9,11},{10,... | collective-permute-start | bytes 3538952 | tf_op jit(solution)/shard_map/ppermute | solution.py:122
  535.9 35.9 %collective-permute-start.31 = (bf16[192,3072]{1,0:T(8,128)(2,1)S(1)}, bf16[192,3072]{1,0:T(8,128)(2,1)S(1)}, u32[]{:S(2)}, u32[]{:S(2)}) collective-permute-start(bf16[192,3072]{1,0:T(8,128)(2,1)S(1)} %get-tuple-element.50), channel_id=1, source_target_pairs={{0,2},{1,3},{2,0},{3,1},{4,6},{5,7},{6,4},{7,5},{8,10},{9,11},{10,... | collective-permute-start | bytes 3538952 | tf_op jit(solution)/shard_map/ppermute | solution.py:122
  551.8 22.1 %collective-permute-start.28 = (bf16[96,3072]{1,0:T(8,128)(2,1)S(1)}, bf16[96,3072]{1,0:T(8,128)(2,1)S(1)}, u32[]{:S(2)}, u32[]{:S(2)}) collective-permute-start(bf16[96,3072]{1,0:T(8,128)(2,1)S(1)} %get-tuple-element.62), channel_id=1, source_target_pairs={{0,4},{1,5},{2,6},{3,7},{4,0},{5,1},{6,2},{7,3},{8,12},{9,13},{10,... | collective-permute-start | bytes 1769480 | tf_op jit(solution)/shard_map/ppermute | solution.py:122
  572.2 16.8 %collective-permute-start.32 = (bf16[96,3072]{1,0:T(8,128)(2,1)S(1)}, bf16[96,3072]{1,0:T(8,128)(2,1)S(1)}, u32[]{:S(2)}, u32[]{:S(2)}) collective-permute-start(bf16[96,3072]{1,0:T(8,128)(2,1)S(1)} %get-tuple-element.60), channel_id=1, source_target_pairs={{0,4},{1,5},{2,6},{3,7},{4,0},{5,1},{6,2},{7,3},{8,12},{9,13},{10,... | collective-permute-start | bytes 1769480 | tf_op jit(solution)/shard_map/ppermute | solution.py:122
  574.1 16.1 %collective-permute-start.29 = (bf16[48,3072]{1,0:T(8,128)(2,1)S(1)}, bf16[48,3072]{1,0:T(8,128)(2,1)S(1)}, u32[]{:S(2)}, u32[]{:S(2)}) collective-permute-start(bf16[48,3072]{1,0:T(8,128)(2,1)S(1)} %add_convert_fusion.25), channel_id=1, source_target_pairs={{0,8},{1,9},{2,10},{3,11},{4,12},{5,13},{6,14},{7,15},{8,0},{9,1},... | collective-permute-start | bytes 884744 | tf_op jit(solution)/shard_map/ppermute | solution.py:122
  589.0 14.5 %collective-permute-start.33 = (bf16[48,3072]{1,0:T(8,128)(2,1)S(1)}, bf16[48,3072]{1,0:T(8,128)(2,1)S(1)}, u32[]{:S(2)}, u32[]{:S(2)}) collective-permute-start(bf16[48,3072]{1,0:T(8,128)(2,1)S(1)} %add_convert_fusion.23), channel_id=1, source_target_pairs={{0,8},{1,9},{2,10},{3,11},{4,12},{5,13},{6,14},{7,15},{8,0},{9,1},... | collective-permute-start | bytes 884744 | tf_op jit(solution)/shard_map/ppermute | solution.py:122
  (207 other events, 957.6 us)
